TPU v7x, 32 devices: a whole 2x2x4 slice. The times are simulated.
32 devices in a mesh: grp: 2 (over x), row: 16 (over z, y, core).
Axes of the slice: x: 2, y: 2, z: 4, core: 2. Of those that a mesh axis runs over, the one named last changes fastest.
Arguments:
- alignment: bfloat16 [128, 128, 256], P(('grp', 'row')), parts along dimension 0, may hold values from -6 to 6
- seq_flags: int32 [128], P(('grp', 'row')), parts along dimension 0, may hold values 0 or 1
- crop_flags: int32 [256], P('grp'), parts along dimension 0, may hold values 0 or 1
- norm_gain: float32 [256], replicated, may hold values from 0.5 to 1.5
- norm_bias: float32 [256], replicated, may hold values from -3 to 3
- left_weight: bfloat16 [256, 32], replicated, may hold values from -0.375 to 0.375
- left_bias: float32 [32], replicated, may hold values from -3 to 3
- right_weight: bfloat16 [256, 32], replicated, may hold values from -0.375 to 0.375
- right_bias: float32 [32], replicated, may hold values from -3 to 3
- out_weight: bfloat16 [1024, 128], replicated, may hold values from -0.1875 to 0.1875
- out_bias: float32 [128], replicated, may hold values from -3 to 3
Outputs:
- pair_update: bfloat16 [256, 128, 128], P(('grp', 'row')), parts along dimension 0
There are 2 independent parts, one for each index of `grp`. A program takes and returns all parts, laid end to end along the dimension named above; an argument that names none is the same for every part. Nothing has to cross between parts.
All inputs are finite; a program needn't handle non-finite values. No bound on the sum of `seq_flags` on one device may be relied on, other than what follows from the above.
Results may differ from a plain program's by a relative error of at most 0.004.
Values may be sent and summed in bfloat16 or wider, within the bound.
A program may use at most 128 MiB of HBM per device.

v0:
```python
import jax
import jax.numpy as jnp
from jax import lax
from jax.sharding import PartitionSpec as P


def normalize(values, norm_gain, norm_bias):
    values = values.astype(jnp.float32)
    average = jnp.mean(values, axis=-1, keepdims=True)
    variance = jnp.mean((values - average) ** 2, axis=-1, keepdims=True)
    return (values - average) * lax.rsqrt(variance + 1e-05) * norm_gain + norm_bias


def project(normed, weight, bias, scaling):
    product = jnp.einsum(
        "src,cd->srd", normed, weight.astype(jnp.float32), precision=lax.Precision.HIGHEST
    )
    return ((product + bias) * scaling).astype(jnp.bfloat16)


def pair_tile(
    left_flat, column_piece, crop_rows, crop_cols, live_count, out_weight, out_bias, channels
):
    rows_here = crop_rows.shape[0]
    width_cols = column_piece.shape[1] // channels
    sums = lax.dot_general(
        left_flat, column_piece, (((0,), (0,)), ((), ())), preferred_element_type=jnp.float32
    )
    outer_sum = sums.reshape(rows_here, channels, width_cols, channels).transpose(0, 2, 1, 3)
    outer_sum = outer_sum.reshape(rows_here * width_cols, channels * channels).astype(jnp.bfloat16)
    projected = jnp.dot(outer_sum, out_weight, preferred_element_type=jnp.float32)
    projected = projected.reshape(rows_here, width_cols, out_weight.shape[1])
    divisor = jnp.maximum(live_count * crop_rows[:, None] * crop_cols[None, :], 1.0)
    return (projected / divisor[:, :, None] + out_bias).astype(jnp.bfloat16)


def column_blocks(
    left_flat, column_piece, crop_rows, crop_cols, live_count, out_weight, out_bias, channels
):
    rows_here = crop_rows.shape[0]
    width_cols = column_piece.shape[1] // channels
    span = max(1, 2048 // rows_here)
    if width_cols > span and width_cols % span == 0:

        def one_block(block_index):
            start = block_index * span
            piece_block = lax.dynamic_slice_in_dim(
                column_piece, start * channels, span * channels, 1
            )
            crop_block = lax.dynamic_slice_in_dim(crop_cols, start, span, 0)
            return pair_tile(
                left_flat,
                piece_block,
                crop_rows,
                crop_block,
                live_count,
                out_weight,
                out_bias,
                channels,
            )

        stacked = lax.map(one_block, jnp.arange(width_cols // span, dtype=jnp.int32))
        return stacked.transpose(1, 0, 2, 3).reshape(rows_here, width_cols, out_weight.shape[1])
    return pair_tile(
        left_flat, column_piece, crop_rows, crop_cols, live_count, out_weight, out_bias, channels
    )


def per_device(
    alignment,
    seq_flags,
    crop_flags,
    norm_gain,
    norm_bias,
    left_weight,
    left_bias,
    right_weight,
    right_bias,
    out_weight,
    out_bias,
):
    channels = left_weight.shape[1]
    devices_row = lax.axis_size("row")
    residues = alignment.shape[1]
    rows_here = residues // devices_row
    crop_float = crop_flags.astype(jnp.float32)
    my_index = lax.axis_index("row")
    crop_rows = lax.dynamic_slice_in_dim(crop_float, my_index * rows_here, rows_here, 0)
    regrouped = lax.all_to_all(alignment, "row", split_axis=1, concat_axis=0, tiled=True)
    all_flags = lax.all_gather(seq_flags, "row", axis=0, tiled=True)
    flag_float = all_flags.astype(jnp.float32)
    live_count = jnp.sum(flag_float)
    normed = normalize(regrouped, norm_gain, norm_bias)
    scaling = flag_float[:, None, None] * crop_rows[None, :, None]
    left = project(normed, left_weight, left_bias, scaling)
    right = project(normed, right_weight, right_bias, scaling)
    sequences = left.shape[0]
    left_flat = left.reshape(sequences, rows_here * channels)
    right_flat = right.reshape(sequences, rows_here * channels)
    return column_blocks(
        left_flat,
        lax.all_gather(right_flat, "row", axis=1, tiled=True),
        crop_rows,
        crop_float,
        live_count,
        out_weight,
        out_bias,
        channels,
    )


def solution(mesh):
    return jax.shard_map(
        per_device,
        mesh=mesh,
        in_specs=(
            P(("grp", "row"), None, None),
            P(("grp", "row")),
            P("grp"),
            P(),
            P(),
            P(),
            P(),
            P(),
            P(),
            P(),
            P(),
        ),
        out_specs=P(("grp", "row"), None, None),
        check_vma=False,
    )
```

profile of v0, /device:TPU:1, one launch (start us, length us, event | category | flops | bytes accessed | tf_op | source)
XLA Modules:
  0.0 54.3 jit_solution(9916558976857848131)
XLA Ops:
  0.0 0.0 copy-start
  0.0 0.0 copy-start.4
  0.0 0.0 copy-start.3
  0.0 1.9 %copy.75 = bf16[4,128,256]{2,0,1:T(4,128)(2,1)} copy(bf16[4,128,256]{2,1,0:T(8,128)(2,1)} %param.11) | data formatting | bytes 524288 | tf_op args[0]
  1.9 7.3 %all-to-all-start = ((bf16[4,128,256]{2,0,1:T(4,128)(2,1)}), bf16[4,128,256]{2,0,1:T(4,128)(2,1)S(1)}, u32[]{:S(2)}, u32[]{:S(2)}) async-start(bf16[4,128,256]{2,0,1:T(4,128)(2,1)} %copy.75), calls=%async_computation | async-start | bytes 524288 | tf_op jit(solution)/shard_map/all_to_all | solution.py:89
  9.3 0.0 copy-start.1
  9.3 0.0 copy-start.5
  9.3 1.3 %dynamic-slice = u32[1]{0:T(128)} dynamic-slice(u32[32]{0:T(128)} %constant.24, u32[]{:T(128)S(6)} %add.58), dynamic_slice_sizes={1} | dynamic-slice | bytes 12
  11.3 0.9 %dynamic-update-slice = s32[64]{0:T(128)S(1)} dynamic-update-slice(s32[64]{0:T(128)S(1)} %broadcast.80, s32[4]{0:T(128)} %param.12, u32[]{:T(128)} %bitcast.7) | dynamic-update-slice | bytes 36
  12.2 9.8 %all-reduce = s32[64]{0:T(128)S(1)} all-reduce(s32[64]{0:T(128)S(1)} %dynamic-update-slice), channel_id=1, replica_groups=mesh['grp'=2,'row'=16] {'row'}, use_global_device_ids=true, to_apply=%add | all-reduce | flops 64 | bytes 512
  22.0 0.7 %convert_reduce_fusion = f32[]{:T(128)} fusion(s32[64]{0:T(128)S(1)} %all-reduce), kind=kLoop, calls=%fused_computation.27 | loop fusion | flops 127 | bytes 260 | tf_op jit(solution)/shard_map/reduce_sum | solution.py:92
  22.7 0.7 %convert_element_type.51 = f32[128]{0:T(128)S(1)} convert(s32[128]{0:T(128)} %param.13) | non-fusion elementwise | flops 128 | bytes 1024 | tf_op jit(solution)/shard_map/convert_element_type | solution.py:86
  23.3 0.8 %broadcast_multiply_fusion.2 = (f32[8]{0:T(128)S(1)}, f32[8]{0:T(128)S(1)}) fusion(f32[]{:T(128)} %convert_reduce_fusion, f32[128]{0:T(128)S(1)} %convert_element_type.51, s32[]{:T(128)S(6)} %select_n.3), kind=kLoop, calls=%fused_computation.26 | loop fusion | flops 8 | bytes 104 | tf_op jit(solution)/shard_map/mul | solution.py:33
  24.1 0.1 multiply_maximum_fusion
  24.2 0.1 broadcast_multiply_fusion
  24.2 0.0 all-to-all-done
  24.3 0.1 fusion.10
  24.4 0.1 copy.79
  24.5 0.1 copy.81
  24.6 0.1 copy.80
  24.6 0.3 multiply_reduce_fusion
  24.9 0.1 copy.83
  25.0 0.1 copy.84
  25.2 0.0 copy-done.4
  25.2 0.0 copy-done.3
  25.2 0.0 copy-start.2
  25.2 0.0 copy-start.6
  25.2 0.2 fusion.9
  25.5 0.0 copy-done.1
  25.5 0.0 copy-done.5
  25.5 0.4 fusion.5
  25.8 0.1 copy.86
  26.0 23.6 %all_gather.7 = bf16[64,4096]{0,1:T(8,128)(2,1)S(1)} all-gather(bf16[64,256]{0,1:T(8,128)(2,1)S(1)} %bitcast.57), channel_id=1, replica_groups=mesh['grp'=2,'row'=16] {'row'}, dimensions={1}, use_global_device_ids=true | all-gather | bytes 557056 | tf_op jit(solution)/shard_map/all_gather | solution.py:102
  49.6 1.1 %copy.87 = bf16[128,32,64]{0,2,1:T(8,128)(2,1)S(1)} copy(bf16[128,32,64]{2,1,0:T(8,128)(2,1)S(1)} %bitcast.55) | data formatting | bytes 1048576 | tf_op jit(solution)/shard_map/dot_general | solution.py:26
  50.7 0.0 copy-done.2
  50.7 0.0 copy-done.6
  50.7 0.4 fusion.4
  51.1 0.1 copy.85
  51.2 0.7 %convert_bitcast_fusion = bf16[8,128,32,32]{1,2,3,0:T(8,128)(2,1)S(1)} fusion(bf16[128,32,64]{0,2,1:T(8,128)(2,1)S(1)} %copy.87, bf16[64,8,32]{0,2,1:T(8,128)(2,1)S(1)} %copy.85), kind=kOutput, calls=%fused_computation | convolution fusion | flops 135266304 | bytes 2654208 | tf_op jit(solution)/shard_map/dot_general | solution.py:26
  51.9 0.0 copy-start.7
  51.9 0.8 %copy.88 = bf16[8,128,32,32]{1,3,2,0:T(8,128)(2,1)S(1)} copy(bf16[8,128,32,32]{1,2,3,0:T(8,128)(2,1)S(1)} %convert_bitcast_fusion) | data formatting | bytes 4194304 | tf_op jit(solution)/shard_map/convert_element_type | solution.py:30
  52.7 0.0 copy-done
  52.7 0.0 copy-done.7
  52.8 1.5 %fusion.1 = bf16[8,128,128]{2,1,0:T(8,128)(2,1)} fusion(bf16[8,128,1024]{1,2,0:T(8,128)(2,1)S(1)} %bitcast.56, bf16[1024,128]{1,0:T(8,128)(2,1)S(1)} %copy-done, f32[128]{0:T(128)S(1)} %copy-done.7, f32[8,128]{1,0:T(8,128)S(1)} %multiply_maximum_fusion), kind=kOutput, calls=%fused_computation.3 | convolution fusion | flops 268828672 | bytes 2626048 | tf_op jit(solution)/shard_map/dot_general | solution.py:31
  (6 shorter events, 0.1 us)
Async XLA Ops:
  0.0 52.7 %copy-start = (bf16[1024,128]{1,0:T(8,128)(2,1)S(1)}, bf16[1024,128]{1,0:T(8,128)(2,1)}, u32[]{:S(2)}) copy-start(bf16[1024,128]{1,0:T(8,128)(2,1)} %param.20) | copy-start | bytes 786436
  0.0 25.2 %copy-start.4 = (f32[256]{0:T(256)S(1)}, f32[256]{0:T(256)}, u32[]{:S(2)}) copy-start(f32[256]{0:T(256)} %param.14) | copy-start | bytes 3076
  0.0 25.2 %copy-start.3 = (f32[256]{0:T(256)S(1)}, f32[256]{0:T(256)}, u32[]{:S(2)}) copy-start(f32[256]{0:T(256)} %param.15) | copy-start | bytes 3076
  1.9 22.3 %all-to-all-start = ((bf16[4,128,256]{2,0,1:T(4,128)(2,1)}), bf16[4,128,256]{2,0,1:T(4,128)(2,1)S(1)}, u32[]{:S(2)}, u32[]{:S(2)}) async-start(bf16[4,128,256]{2,0,1:T(4,128)(2,1)} %copy.75), calls=%async_computation | async-start | bytes 524288 | tf_op jit(solution)/shard_map/all_to_all | solution.py:89
  9.3 16.2 %copy-start.1 = (bf16[256,32]{0,1:T(8,128)(2,1)S(1)}, bf16[256,32]{0,1:T(8,128)(2,1)}, u32[]{:S(2)}) copy-start(bf16[256,32]{0,1:T(8,128)(2,1)} %param.18) | copy-start | bytes 49156
  9.3 16.2 %copy-start.5 = (f32[32]{0:T(128)S(1)}, f32[32]{0:T(128)}, u32[]{:S(2)}) copy-start(f32[32]{0:T(128)} %param.19) | copy-start | bytes 388
  25.2 25.5 %copy-start.2 = (bf16[256,32]{0,1:T(8,128)(2,1)S(1)}, bf16[256,32]{0,1:T(8,128)(2,1)}, u32[]{:S(2)}) copy-start(bf16[256,32]{0,1:T(8,128)(2,1)} %param.16) | copy-start | bytes 49156
  25.2 25.5 %copy-start.6 = (f32[32]{0:T(128)S(1)}, f32[32]{0:T(128)}, u32[]{:S(2)}) copy-start(f32[32]{0:T(128)} %param.17) | copy-start | bytes 388
  51.9 0.8 %copy-start.7 = (f32[128]{0:T(128)S(1)}, f32[128]{0:T(128)}, u32[]{:S(2)}) copy-start(f32[128]{0:T(128)} %param.21) | copy-start | bytes 1540
where the time goes:
time: 54.7 us; the launch traced here: 54.3 us
  blocking collectives  33.4 us (61%)
  starting transfers between devices  7.35 us (13%)
  local copies, waits for them, and re-layouts  6.75 us (12%)
  other arithmetic  2.94 us (5%)
  matrix products  2.91 us (5%)
  between operations  0.89 us (2%)
    all_gather x1, blocking collectives, per_device(): lax.all_gather(right_flat, 'row', axis=1, tiled=True)  23.6 us
    unnamed x1, blocking collectives  9.82 us
    all_to_all x1, starting transfers between devices, per_device(): lax.all_to_all(alignment, 'row', split_axis=1, concat_axis=0, tiled=True)  7.35 us
    unnamed x20, local copies, waits for them, and re-layouts  4.12 us
    dot_general x1, matrix products, pair_tile(): jnp.dot(outer_sum, out_weight, preferred_element_type=jnp.float32)  1.49 us
    dot_general x1, local copies, waits for them, and re-layouts, pair_tile(): lax.dot_general(left_flat, column_piece, (((0,), (0,)), ((), ())), prefer...  1.11 us
  transfers between devices with their start and end apart: 1, of which 0 were waited for; matrix products, arithmetic and copies ran while one was open for 8% of the time, Pallas kernels for 0%

commit v1 on v0

v1 whole, which is shorter than its diff:
```python
import functools

import jax
import jax.numpy as jnp
from jax import lax
from jax.experimental import pallas as pl
from jax.experimental.pallas import tpu as pltpu
from jax.sharding import PartitionSpec as P

LANES = 128
TILE = 16


def copy_plan(steps):
    plan = []
    for a in range(1, steps):
        plan.append(("left", a))
        plan.append(("main", a))
    for a in range(steps):
        plan.append(("side", a))
    for b in range(2):
        for a in range(steps):
            plan.append(("twin", a, b))
    return {name: number for number, name in enumerate(plan)}


def kernel(
    steps,
    flags_ref,
    crop_smem,
    x_ref,
    crop_ref,
    gain_ref,
    shift_ref,
    lw_ref,
    lb_ref,
    rw_ref,
    rb_ref,
    ow_ref,
    ob_ref,
    out_ref,
    held,
    left_src,
    right_f32,
    left_f32,
    weight_f32,
    weight_t,
    outer,
    send_sem,
    recv_sem,
    recv_left,
):
    seqs, residues, width = x_ref.shape
    channels = lw_ref.shape[0]
    rows_here = out_ref.shape[0]
    pair = out_ref.shape[2]
    count = steps * 4
    blocks = residues // LANES
    left_rows = 4 * rows_here
    head = left_rows + TILE
    block_rows = seqs * channels
    total_rows = held.shape[3]
    plan = copy_plan(steps)

    me = lax.axis_index("row")
    core = lax.rem(me, 2)
    side = lax.rem(lax.div(me, 2), 2)
    line = lax.div(me, 4)

    def at_line(offset):
        return lax.rem(line + offset, steps) * 4 + side * 2 + core

    twin = me + 1 - 2 * core
    across = me + 2 - 4 * side

    barrier = pltpu.get_barrier_semaphore()
    peers = [at_line(a) for a in range(1, steps)] + [across, twin]
    for peer in peers:
        pl.semaphore_signal(
            barrier, inc=1, device_id={"row": peer}, device_id_type=pl.DeviceIdType.MESH
        )

    def copy(src, dst, name, recv, device):
        return pltpu.make_async_remote_copy(
            src_ref=src,
            dst_ref=dst,
            send_sem=send_sem.at[plan[name]],
            recv_sem=recv,
            device_id={"row": device},
            device_id_type=pl.DeviceIdType.MESH,
        )

    values = x_ref[...].astype(jnp.float32).reshape(seqs * residues, width)
    average = jnp.mean(values, axis=-1, keepdims=True)
    centred = values - average
    variance = jnp.mean(centred * centred, axis=-1, keepdims=True)
    normed = centred * lax.rsqrt(variance + 1e-05) * gain_ref[...] + shift_ref[...]
    high = normed.astype(jnp.bfloat16)
    low = (normed - high.astype(jnp.float32)).astype(jnp.bfloat16)

    def dot_t(a, b):
        return lax.dot_general(a, b, (((1,), (1,)), ((), ())), preferred_element_type=jnp.float32)

    right = dot_t(rw_ref[...], high) + dot_t(rw_ref[...], low)
    row_of = lax.broadcasted_iota(jnp.int32, (channels, channels), 0)
    col_of = lax.broadcasted_iota(jnp.int32, (channels, channels), 1)
    right_bias = jnp.sum(jnp.where(row_of == col_of, rb_ref[...], 0.0), axis=1, keepdims=True)
    right = right + right_bias
    lane_of = lax.broadcasted_iota(jnp.int32, (TILE, LANES), 1)
    row_id = lax.broadcasted_iota(jnp.int32, (TILE, LANES), 0)
    flag_tile = jnp.zeros((TILE, LANES), jnp.float32)
    for s in range(seqs):
        flag = flags_ref[s].astype(jnp.float32)
        flag_tile = jnp.where((lane_of == s % LANES) & (row_id == s // LANES), flag, flag_tile)
        for b in range(blocks):
            start = s * residues + b * LANES
            piece = (right[:, start : start + LANES] * flag).astype(jnp.bfloat16)
            place = head + b * block_rows + s * channels
            held[0, 0, 0, place : place + channels, :] = piece
    held[0, 0, 0, left_rows:head, :] = flag_tile.astype(jnp.bfloat16)

    left = dot_t(high, lw_ref[...]) + dot_t(low, lw_ref[...]) + lb_ref[...]
    left = jnp.concatenate(
        [left[s * residues : (s + 1) * residues, :] for s in range(seqs)], axis=1
    )
    left_src[...] = left.astype(jnp.bfloat16)
    own = pl.multiple_of(line * left_rows, left_rows)
    held[0, 0, 0, 0:left_rows, :] = left_src[pl.ds(own, left_rows), :]

    pl.semaphore_wait(barrier, len(peers))

    main = pl.ds(left_rows, total_rows - left_rows)
    upper = pl.ds(0, left_rows)
    started = []

    def left_copy(a):
        there = lax.rem(line + a, steps)
        rows = pl.ds(pl.multiple_of(there * left_rows, left_rows), left_rows)
        slot = (steps - a) % steps
        return copy(
            left_src.at[rows, :],
            held.at[slot, 0, 0, upper, :],
            ("left", a),
            recv_left.at[slot],
            at_line(a),
        )

    def main_copy(a):
        slot = (steps - a) % steps
        return copy(
            held.at[0, 0, 0, main, :],
            held.at[slot, 0, 0, main, :],
            ("main", a),
            recv_sem.at[slot, 0, 0],
            at_line(a),
        )

    def side_copy(a):
        return copy(
            held.at[a, 0, 0], held.at[a, 1, 0], ("side", a), recv_sem.at[a, 1, 0], across
        )

    def twin_copy(a, b):
        return copy(
            held.at[a, b, 0], held.at[a, b, 1], ("twin", a, b), recv_sem.at[a, b, 1], twin
        )

    def launch(one):
        one.start()
        started.append(one)

    def absorb(a, b, c):
        k = (c * 2 + b) * steps + a
        for j in range(blocks):
            rows = held[a, b, c, head + j * block_rows : head + (j + 1) * block_rows, :]
            base = (j * count + k) * block_rows
            right_f32[base : base + block_rows, :] = rows.astype(jnp.float32)
        start = pl.multiple_of(side * 2 * rows_here, 2 * rows_here)
        mine = held[a, b, c, pl.ds(start, 2 * rows_here), :].astype(jnp.float32)
        mine = jnp.where(core == 0, mine[:rows_here, :], mine[rows_here:, :])
        left_f32[k * rows_here : (k + 1) * rows_here, :] = mine
        return held[a, b, c, left_rows:head, :].astype(jnp.float32)

    launch(side_copy(0))
    for a in range(1, steps):
        launch(left_copy(a))
        launch(main_copy(a))
    launch(twin_copy(0, 0))
    flags = absorb(0, 0, 0)

    weight_f32[...] = ow_ref[...].astype(jnp.float32)
    for e in range(channels):
        part = weight_f32[pl.ds(e, channels, stride=channels), :]
        outer[e * channels : (e + 1) * channels, 0:pair] = part.astype(jnp.bfloat16)
    weight_t[...] = outer[:, 0:pair].astype(jnp.float32).T.astype(jnp.bfloat16)

    for a in range(1, steps):
        left_copy(steps - a).wait_recv()
        main_copy(steps - a).wait_recv()
        launch(side_copy(a))
        launch(twin_copy(a, 0))
        flags = flags + absorb(a, 0, 0)
    for a in range(steps):
        side_copy(a).wait_recv()
        launch(twin_copy(a, 1))
        flags = flags + absorb(a, 1, 0)
    for b in range(2):
        for a in range(steps):
            twin_copy(a, b).wait_recv()
            flags = flags + absorb(a, b, 1)

    live = jnp.sum(jnp.sum(flags, axis=0, keepdims=True), axis=1, keepdims=True)

    ordered = jnp.concatenate(
        [left_f32[pl.ds(i, count, stride=rows_here), :] for i in range(rows_here)], axis=0
    )
    turned = ordered.T
    left_all = jnp.concatenate(
        [
            jnp.concatenate(
                [
                    turned[s * channels : (s + 1) * channels, i * count : (i + 1) * count]
                    for s in range(seqs)
                ],
                axis=1,
            )
            for i in range(rows_here)
        ],
        axis=0,
    ).astype(jnp.bfloat16)

    for j in range(blocks):
        for e in range(channels):
            base = j * count * block_rows
            piece = jnp.concatenate(
                [
                    right_f32[pl.ds(base + s * channels + e, count, stride=block_rows), :]
                    for s in range(seqs)
                ],
                axis=0,
            ).astype(jnp.bfloat16)
            sums = jnp.dot(left_all, piece, preferred_element_type=jnp.float32)
            sums = sums.astype(jnp.bfloat16)
            for i in range(rows_here):
                outer[e * channels : (e + 1) * channels, i * LANES : (i + 1) * LANES] = sums[
                    i * channels : (i + 1) * channels, :
                ]
        crop_cols = crop_ref[:, j * LANES : (j + 1) * LANES].astype(jnp.float32)
        projected = jnp.dot(weight_t[...], outer[...], preferred_element_type=jnp.float32)
        for i in range(rows_here):
            mask = crop_smem[me * rows_here + i].astype(jnp.float32) * crop_cols
            scale = mask / jnp.maximum(live * mask, 1.0)
            block = projected[:, i * LANES : (i + 1) * LANES] * scale
            out_ref[i, j * LANES : (j + 1) * LANES, :] = (block.T + ob_ref[...]).astype(
                out_ref.dtype
            )

    for one in started:
        one.wait_send()


def per_device(
    alignment,
    seq_flags,
    crop_flags,
    norm_gain,
    norm_bias,
    left_weight,
    left_bias,
    right_weight,
    right_bias,
    out_weight,
    out_bias,
):
    devices = lax.axis_size("row")
    steps = devices // 4
    seqs, residues, _ = alignment.shape
    channels = left_weight.shape[1]
    pair = out_weight.shape[1]
    rows_here = residues // devices
    block_rows = seqs * channels
    total_rows = 4 * rows_here + TILE + block_rows * (residues // LANES)
    vmem = pl.BlockSpec(memory_space=pltpu.VMEM)
    smem = pl.BlockSpec(memory_space=pltpu.SMEM)
    return pl.pallas_call(
        functools.partial(kernel, steps),
        out_shape=jax.ShapeDtypeStruct((rows_here, residues, pair), jnp.bfloat16),
        in_specs=[smem, smem] + [vmem] * 10,
        out_specs=vmem,
        scratch_shapes=[
            pltpu.VMEM((steps, 2, 2, total_rows, LANES), jnp.bfloat16),
            pltpu.VMEM((residues, seqs * channels), jnp.bfloat16),
            pltpu.VMEM((residues // LANES * devices * block_rows, LANES), jnp.float32),
            pltpu.VMEM((devices * rows_here, seqs * channels), jnp.float32),
            pltpu.VMEM((channels * channels, pair), jnp.float32),
            pltpu.VMEM((pair, channels * channels), jnp.bfloat16),
            pltpu.VMEM((channels * channels, rows_here * LANES), jnp.bfloat16),
            pltpu.SemaphoreType.DMA((len(copy_plan(steps)),)),
            pltpu.SemaphoreType.DMA((steps, 2, 2)),
            pltpu.SemaphoreType.DMA((steps,)),
        ],
        compiler_params=pltpu.CompilerParams(
            collective_id=0, has_side_effects=True, vmem_limit_bytes=48 * 1024 * 1024
        ),
    )(
        seq_flags,
        crop_flags,
        alignment,
        crop_flags.reshape(1, residues),
        norm_gain.reshape(1, -1),
        norm_bias.reshape(1, -1),
        left_weight.T,
        left_bias.reshape(1, -1),
        right_weight.T,
        right_bias.reshape(1, -1),
        out_weight,
        out_bias.reshape(1, -1),
    )


def solution(mesh):
    return jax.shard_map(
        per_device,
        mesh=mesh,
        in_specs=(
            P(("grp", "row"), None, None),
            P(("grp", "row")),
            P("grp"),
            P(),
            P(),
            P(),
            P(),
            P(),
            P(),
            P(),
            P(),
        ),
        out_specs=P(("grp", "row"), None, None),
        check_vma=False,
    )
```

time: 54.7 us -> 22.3 us (0.41)
  blocking collectives: 33.4 us -> 0 us
  Pallas kernels: 0 us -> 17.1 us
  starting transfers between devices: 7.35 us -> 0 us
  other arithmetic: 2.94 us -> 0 us
  matrix products: 2.91 us -> 0 us
  local copies, waits for them, and re-layouts: 6.75 us -> 4.77 us
  between operations: 0.89 us -> 0.05 us
    all_gather x1 -> x0, blocking collectives: 23.6 us -> none  [per_device(): lax.all_gather(right_flat, 'row', axis=1, tiled=True)]
    pallas_call x0 -> x1, Pallas kernels: none -> 17.1 us  [per_device(): pl.pallas_call(functools.partial(kernel, steps), out_shape=jax.ShapeDtype...]
    unnamed x1 -> x0, blocking collectives: 9.82 us -> none
    all_to_all x1 -> x0, starting transfers between devices: 7.35 us -> none  [per_device(): lax.all_to_all(alignment, 'row', split_axis=1, concat_axis=0, tiled=True)]
    dot_general x4 -> x0, matrix products: 2.91 us -> none  [the longest x1 1.49 us: pair_tile(): jnp.dot(outer_sum, out_weight, preferred_element_type=jnp.float32)]
    convert_element_type x4 -> x0, local copies, waits for them, and re-layouts: 1.14 us -> none  [the longest x1 0.82 us: pair_tile(): outer_sum.reshape(rows_here * width_cols, channels * channels)]
    dot_general x1 -> x0, local copies, waits for them, and re-layouts: 1.11 us -> none  [pair_tile(): lax.dot_general(left_flat, column_piece, (((0,), (0,)), ((), ())), prefer...]
    reduce_sum x3 -> x0, other arithmetic: 1.1 us -> none  [the longest x1 0.68 us: per_device(): live_count = jnp.sum(flag_float)]
  transfers between devices with their start and end apart: 1 -> 0, of which waited for: 0 -> 0; matrix products, arithmetic and copies ran while one was open for 8% -> 0% of each run, Pallas kernels for 0% -> 0%
where the time goes in v1:
time: 22.3 us; the launch traced here: 21.9 us
  Pallas kernels  17.1 us (77%)
  local copies, waits for them, and re-layouts  4.77 us (21%)
    pallas_call x1, Pallas kernels, per_device(): pl.pallas_call(functools.partial(kernel, steps), out_shape=jax.ShapeDtype...  17.1 us
    unnamed x23, local copies, waits for them, and re-layouts  4.77 us

profile of v1, /device:TPU:1, one launch (start us, length us, event | category | flops | bytes accessed | tf_op | source)
XLA Modules:
  0.0 21.9 jit_solution(2844244693361075024)
XLA Ops:
  0.0 0.0 copy-start.9
  0.0 0.0 copy-start.10
  0.0 0.0 copy-start.6
  0.0 0.0 copy-start.7
  0.0 0.0 copy-start.8
  0.0 0.0 copy-start.4
  0.0 0.0 copy-start.5
  0.0 0.6 %copy-done.9 = f32[32]{0:T(128)S(1)} copy-done((f32[32]{0:T(128)S(1)}, f32[32]{0:T(128)}, u32[]{:S(2)}) %copy-start.9) | copy-done | bytes 152
  0.7 0.0 copy-done.10
  0.7 0.0 copy-done.6
  0.7 0.0 copy-done.7
  0.7 0.0 copy-done.8
  0.7 0.0 copy-done.4
  0.7 0.0 copy-done.5
  0.8 0.0 copy-start
  0.8 0.9 %copy-done = bf16[4,128,256]{2,1,0:T(8,128)(2,1)S(1)} copy-done((bf16[4,128,256]{2,1,0:T(8,128)(2,1)S(1)}, bf16[4,128,256]{2,1,0:T(8,128)(2,1)}, u32[]{:S(2)}) %copy-start) | copy-done | bytes 262168
  1.7 0.0 copy-start.1
  1.7 0.9 %copy-done.1 = bf16[1024,128]{1,0:T(8,128)(2,1)S(1)} copy-done((bf16[1024,128]{1,0:T(8,128)(2,1)S(1)}, bf16[1024,128]{1,0:T(8,128)(2,1)}, u32[]{:S(2)}) %copy-start.1) | copy-done | bytes 262168
  2.7 0.0 copy-start.2
  2.7 0.7 %copy-done.2 = bf16[256,32]{0,1:T(8,128)(2,1)S(1)} copy-done((bf16[256,32]{0,1:T(8,128)(2,1)S(1)}, bf16[256,32]{0,1:T(8,128)(2,1)}, u32[]{:S(2)}) %copy-start.2) | copy-done | bytes 16408
  3.4 0.0 copy-start.3
  3.4 0.7 %copy-done.3 = bf16[256,32]{0,1:T(8,128)(2,1)S(1)} copy-done((bf16[256,32]{0,1:T(8,128)(2,1)S(1)}, bf16[256,32]{0,1:T(8,128)(2,1)}, u32[]{:S(2)}) %copy-start.3) | copy-done | bytes 16408
  4.1 17.1 %shard_map.109 = bf16[8,128,128]{2,1,0:T(8,128)(2,1)S(1)} custom-call(s32[4]{0:T(128)S(1)} %copy-done.7, s32[128]{0:T(128)S(1)} %copy-done.4, bf16[4,128,256]{2,1,0:T(8,128)(2,1)S(1)} %copy-done, s32[1,128]{1,0:T(1,128)S(1)} %bitcast.10, f32[1,256]{1,0:T(1,128)S(1)} %bitcast.11, f32[1,256]{1,0:T(1,128)S(1)} %bitcast.12, bf16[32,256]{1,0:T(8,128)(2,1)S(1)} %bitcast.8, ...), custom_call_target="tpu_custom_call" | custom-call | tf_op jit(solution)/shard_map/pallas_call | solution.py:285
  21.2 0.7 %copy.13 = bf16[8,128,128]{2,1,0:T(8,128)(2,1)} copy(bf16[8,128,128]{2,1,0:T(8,128)(2,1)S(1)} %shard_map.109) | data formatting | bytes 524288
Async XLA Ops:
  0.0 0.7 %copy-start.9 = (f32[32]{0:T(128)S(1)}, f32[32]{0:T(128)}, u32[]{:S(2)}) copy-start(f32[32]{0:T(128)} %param.19) | copy-start | bytes 388
  0.0 0.7 %copy-start.10 = (f32[128]{0:T(128)S(1)}, f32[128]{0:T(128)}, u32[]{:S(2)}) copy-start(f32[128]{0:T(128)} %param.21) | copy-start | bytes 1540
  0.0 0.7 %copy-start.6 = (f32[256]{0:T(256)S(1)}, f32[256]{0:T(256)}, u32[]{:S(2)}) copy-start(f32[256]{0:T(256)} %param.15) | copy-start | bytes 3076
  0.0 0.7 %copy-start.7 = (s32[4]{0:T(128)S(1)}, s32[4]{0:T(128)}, u32[]{:S(2)}) copy-start(s32[4]{0:T(128)} %flags_ref.1) | copy-start | bytes 52
  0.0 0.7 %copy-start.8 = (f32[32]{0:T(128)S(1)}, f32[32]{0:T(128)}, u32[]{:S(2)}) copy-start(f32[32]{0:T(128)} %param.17) | copy-start | bytes 388
  0.0 0.7 %copy-start.4 = (s32[128]{0:T(128)S(1)}, s32[128]{0:T(128)}, u32[]{:S(2)}) copy-start(s32[128]{0:T(128)} %crop_smem.1) | copy-start | bytes 1540
  0.0 0.7 %copy-start.5 = (f32[256]{0:T(256)S(1)}, f32[256]{0:T(256)}, u32[]{:S(2)}) copy-start(f32[256]{0:T(256)} %param.14) | copy-start | bytes 3076
  0.8 0.9 %copy-start = (bf16[4,128,256]{2,1,0:T(8,128)(2,1)S(1)}, bf16[4,128,256]{2,1,0:T(8,128)(2,1)}, u32[]{:S(2)}) copy-start(bf16[4,128,256]{2,1,0:T(8,128)(2,1)} %x_ref.1) | copy-start | bytes 786436
  1.7 0.9 %copy-start.1 = (bf16[1024,128]{1,0:T(8,128)(2,1)S(1)}, bf16[1024,128]{1,0:T(8,128)(2,1)}, u32[]{:S(2)}) copy-start(bf16[1024,128]{1,0:T(8,128)(2,1)} %ow_ref.1) | copy-start | bytes 786436
  2.7 0.7 %copy-start.2 = (bf16[256,32]{0,1:T(8,128)(2,1)S(1)}, bf16[256,32]{0,1:T(8,128)(2,1)}, u32[]{:S(2)}) copy-start(bf16[256,32]{0,1:T(8,128)(2,1)} %param.16) | copy-start | bytes 49156
  3.4 0.7 %copy-start.3 = (bf16[256,32]{0,1:T(8,128)(2,1)S(1)}, bf16[256,32]{0,1:T(8,128)(2,1)}, u32[]{:S(2)}) copy-start(bf16[256,32]{0,1:T(8,128)(2,1)} %param.18) | copy-start | bytes 49156

commit v2 on v1

--- a/solution.py
+++ b/solution.py
@@ -9,6 +9,7 @@
 
 LANES = 128
 TILE = 16
+INPUTS = 12
 
 
 def copy_plan(steps):
@@ -26,30 +27,43 @@
 
 def kernel(
     steps,
-    flags_ref,
-    crop_smem,
-    x_ref,
-    crop_ref,
-    gain_ref,
-    shift_ref,
-    lw_ref,
-    lb_ref,
-    rw_ref,
-    rb_ref,
-    ow_ref,
-    ob_ref,
-    out_ref,
-    held,
-    left_src,
-    right_f32,
-    left_f32,
-    weight_f32,
-    weight_t,
-    outer,
-    send_sem,
-    recv_sem,
-    recv_left,
+    *refs,
 ):
+    sources, out_ref, refs = refs[:INPUTS], refs[INPUTS], refs[INPUTS + 1 :]
+    inputs, refs = refs[:INPUTS], refs[INPUTS:]
+    (
+        x_ref,
+        gain_ref,
+        shift_ref,
+        rw_ref,
+        rb_ref,
+        lw_ref,
+        lb_ref,
+        flags_ref,
+        ow_ref,
+        crop_smem,
+        crop_ref,
+        ob_ref,
+    ) = inputs
+    (
+        held,
+        left_src,
+        right_f32,
+        left_f32,
+        weight_f32,
+        weight_t,
+        outer,
+        send_sem,
+        recv_sem,
+        recv_left,
+        load_sem,
+    ) = refs
+    loads = [
+        pltpu.make_async_copy(source, there, load_sem.at[number])
+        for number, (source, there) in enumerate(zip(sources, inputs))
+    ]
+    for load in loads:
+        load.start()
     seqs, residues, width = x_ref.shape
     channels = lw_ref.shape[0]
     rows_here = out_ref.shape[0]
@@ -90,6 +104,8 @@
             device_id_type=pl.DeviceIdType.MESH,
         )
 
+    for load in loads[:8]:
+        load.wait()
     values = x_ref[...].astype(jnp.float32).reshape(seqs * residues, width)
     average = jnp.mean(values, axis=-1, keepdims=True)
     centred = values - average
@@ -188,6 +204,8 @@
     launch(twin_copy(0, 0))
     flags = absorb(0, 0, 0)
 
+    for load in loads[8:]:
+        load.wait()
     weight_f32[...] = ow_ref[...].astype(jnp.float32)
     for e in range(channels):
         part = weight_f32[pl.ds(e, channels, stride=channels), :]
@@ -280,14 +298,29 @@
     rows_here = residues // devices
     block_rows = seqs * channels
     total_rows = 4 * rows_here + TILE + block_rows * (residues // LANES)
-    vmem = pl.BlockSpec(memory_space=pltpu.VMEM)
-    smem = pl.BlockSpec(memory_space=pltpu.SMEM)
+    operands = [
+        alignment,
+        norm_gain.reshape(1, -1),
+        norm_bias.reshape(1, -1),
+        right_weight.T,
+        right_bias.reshape(1, -1),
+        left_weight.T,
+        left_bias.reshape(1, -1),
+        seq_flags,
+        out_weight,
+        crop_flags,
+        crop_flags.reshape(1, residues),
+        out_bias.reshape(1, -1),
+    ]
+    spaces = [pltpu.VMEM] * INPUTS
+    spaces[7] = spaces[9] = pltpu.SMEM
     return pl.pallas_call(
         functools.partial(kernel, steps),
         out_shape=jax.ShapeDtypeStruct((rows_here, residues, pair), jnp.bfloat16),
-        in_specs=[smem, smem] + [vmem] * 10,
-        out_specs=vmem,
-        scratch_shapes=[
+        in_specs=[pl.BlockSpec(memory_space=pltpu.HBM)] * INPUTS,
+        out_specs=pl.BlockSpec(memory_space=pltpu.VMEM),
+        scratch_shapes=[space(one.shape, one.dtype) for space, one in zip(spaces, operands)]
+        + [
             pltpu.VMEM((steps, 2, 2, total_rows, LANES), jnp.bfloat16),
             pltpu.VMEM((residues, seqs * channels), jnp.bfloat16),
             pltpu.VMEM((residues // LANES * devices * block_rows, LANES), jnp.float32),
@@ -298,24 +331,12 @@
             pltpu.SemaphoreType.DMA((len(copy_plan(steps)),)),
             pltpu.SemaphoreType.DMA((steps, 2, 2)),
             pltpu.SemaphoreType.DMA((steps,)),
+            pltpu.SemaphoreType.DMA((INPUTS,)),
         ],
         compiler_params=pltpu.CompilerParams(
-            collective_id=0, has_side_effects=True, vmem_limit_bytes=48 * 1024 * 1024
+            collective_id=0, has_side_effects=True, vmem_limit_bytes=60 * 1024 * 1024
         ),
-    )(
-        seq_flags,
-        crop_flags,
-        alignment,
-        crop_flags.reshape(1, residues),
-        norm_gain.reshape(1, -1),
-        norm_bias.reshape(1, -1),
-        left_weight.T,
-        left_bias.reshape(1, -1),
-        right_weight.T,
-        right_bias.reshape(1, -1),
-        out_weight,
-        out_bias.reshape(1, -1),
-    )
+    )(*operands)
 
 
 def solution(mesh):

time: 22.3 us -> 18.8 us (0.84)
  local copies, waits for them, and re-layouts: 4.77 us -> 1.67 us
    unnamed x23 -> x1, local copies, waits for them, and re-layouts: 4.77 us -> 1.67 us
where the time goes in v2:
time: 18.8 us; the launch traced here: 18.6 us
  Pallas kernels  16.9 us (90%)
  local copies, waits for them, and re-layouts  1.67 us (9%)
    pallas_call x1, Pallas kernels, per_device(): pl.pallas_call(functools.partial(kernel, steps), out_shape=jax.ShapeDtype...  16.9 us
    unnamed x1, local copies, waits for them, and re-layouts  1.67 us

profile of v2, /device:TPU:1, one launch (start us, length us, event | category | flops | bytes accessed | tf_op | source)
XLA Modules:
  0.0 18.6 jit_solution(2505994052360858784)
XLA Ops:
  0.0 16.9 %shard_map.109 = bf16[8,128,128]{2,1,0:T(8,128)(2,1)} custom-call(bf16[4,128,256]{2,1,0:T(8,128)(2,1)} %refs_0_.1, f32[1,256]{1,0:T(1,128)} %bitcast.11, f32[1,256]{1,0:T(1,128)} %bitcast.12, bf16[32,256]{1,0:T(8,128)(2,1)} %bitcast.8, f32[1,32]{1,0:T(1,128)} %bitcast.13, bf16[32,256]{1,0:T(8,128)(2,1)} %bitcast.9, f32[1,32]{1,0:T(1,128)} %bitcast.14, ...), custom_call_target="tpu_custom_call" | custom-call | tf_op jit(solution)/shard_map/pallas_call | solution.py:317
  16.9 1.7 %copy.13 = bf16[8,128,128]{2,1,0:T(8,128)(2,1)} copy(bf16[8,128,128]{2,1,0:T(8,128)(2,1)} %shard_map.109) | data formatting | bytes 524288

commit v3 on v2

--- a/solution.py
+++ b/solution.py
@@ -71,7 +71,9 @@
     count = steps * 4
     blocks = residues // LANES
     left_rows = 4 * rows_here
-    head = left_rows + TILE
+    near = (steps - 1) * left_rows
+    flag_row = steps * left_rows
+    head = flag_row + TILE
     block_rows = seqs * channels
     total_rows = held.shape[3]
     plan = copy_plan(steps)
@@ -81,14 +83,24 @@
     side = lax.rem(lax.div(me, 2), 2)
     line = lax.div(me, 4)
 
-    def at_line(offset):
-        return lax.rem(line + offset, steps) * 4 + side * 2 + core
+    def other(bits):
+        there = line
+        bit = 1
+        while bit <= bits:
+            if bits & bit:
+                there = there + bit - 2 * bit * lax.rem(lax.div(there, bit), 2)
+            bit *= 2
+        return there
+
+    def at_line(bits):
+        return other(bits) * 4 + side * 2 + core
 
     twin = me + 1 - 2 * core
     across = me + 2 - 4 * side
 
     barrier = pltpu.get_barrier_semaphore()
-    peers = [at_line(a) for a in range(1, steps)] + [across, twin]
+    hops = [1 << t for t in range(steps.bit_length() - 1)]
+    peers = [at_line(bit) for bit in hops] + [across, twin]
     for peer in peers:
         pl.semaphore_signal(
             barrier, inc=1, device_id={"row": peer}, device_id_type=pl.DeviceIdType.MESH
@@ -133,52 +145,60 @@
             piece = (right[:, start : start + LANES] * flag).astype(jnp.bfloat16)
             place = head + b * block_rows + s * channels
             held[0, 0, 0, place : place + channels, :] = piece
-    held[0, 0, 0, left_rows:head, :] = flag_tile.astype(jnp.bfloat16)
+    held[0, 0, 0, flag_row:head, :] = flag_tile.astype(jnp.bfloat16)
 
     left = dot_t(high, lw_ref[...]) + dot_t(low, lw_ref[...]) + lb_ref[...]
     left = jnp.concatenate(
         [left[s * residues : (s + 1) * residues, :] for s in range(seqs)], axis=1
     )
     left_src[...] = left.astype(jnp.bfloat16)
-    own = pl.multiple_of(line * left_rows, left_rows)
-    held[0, 0, 0, 0:left_rows, :] = left_src[pl.ds(own, left_rows), :]
+    for q in range(steps):
+        start = pl.multiple_of(other(q) * left_rows, left_rows)
+        place = (steps - 1 - q) * left_rows
+        held[0, 0, 0, place : place + left_rows, :] = left_src[pl.ds(start, left_rows), :]
 
     pl.semaphore_wait(barrier, len(peers))
 
-    main = pl.ds(left_rows, total_rows - left_rows)
-    upper = pl.ds(0, left_rows)
+    main = pl.ds(flag_row, total_rows - flag_row)
+    tail = pl.ds(near, total_rows - near)
     started = []
 
     def left_copy(a):
-        there = lax.rem(line + a, steps)
-        rows = pl.ds(pl.multiple_of(there * left_rows, left_rows), left_rows)
-        slot = (steps - a) % steps
+        bit = a & -a
         return copy(
-            left_src.at[rows, :],
-            held.at[slot, 0, 0, upper, :],
+            held.at[a - bit, 0, 0, pl.ds((steps - 2 * bit) * left_rows, bit * left_rows), :],
+            held.at[a, 0, 0, pl.ds((steps - bit) * left_rows, bit * left_rows), :],
             ("left", a),
-            recv_left.at[slot],
-            at_line(a),
+            recv_left.at[a],
+            at_line(bit),
         )
 
     def main_copy(a):
-        slot = (steps - a) % steps
+        bit = a & -a
         return copy(
-            held.at[0, 0, 0, main, :],
-            held.at[slot, 0, 0, main, :],
+            held.at[a - bit, 0, 0, main, :],
+            held.at[a, 0, 0, main, :],
             ("main", a),
-            recv_sem.at[slot, 0, 0],
-            at_line(a),
+            recv_sem.at[a, 0, 0],
+            at_line(bit),
         )
 
     def side_copy(a):
         return copy(
-            held.at[a, 0, 0], held.at[a, 1, 0], ("side", a), recv_sem.at[a, 1, 0], across
+            held.at[a, 0, 0, tail, :],
+            held.at[a, 1, 0, tail, :],
+            ("side", a),
+            recv_sem.at[a, 1, 0],
+            across,
         )
 
     def twin_copy(a, b):
         return copy(
-            held.at[a, b, 0], held.at[a, b, 1], ("twin", a, b), recv_sem.at[a, b, 1], twin
+            held.at[a, b, 0, tail, :],
+            held.at[a, b, 1, tail, :],
+            ("twin", a, b),
+            recv_sem.at[a, b, 1],
+            twin,
         )
 
     def launch(one):
@@ -191,17 +211,22 @@
             rows = held[a, b, c, head + j * block_rows : head + (j + 1) * block_rows, :]
             base = (j * count + k) * block_rows
             right_f32[base : base + block_rows, :] = rows.astype(jnp.float32)
-        start = pl.multiple_of(side * 2 * rows_here, 2 * rows_here)
+        start = pl.multiple_of(near + side * 2 * rows_here, 2 * rows_here)
         mine = held[a, b, c, pl.ds(start, 2 * rows_here), :].astype(jnp.float32)
         mine = jnp.where(core == 0, mine[:rows_here, :], mine[rows_here:, :])
         left_f32[k * rows_here : (k + 1) * rows_here, :] = mine
-        return held[a, b, c, left_rows:head, :].astype(jnp.float32)
-
-    launch(side_copy(0))
-    for a in range(1, steps):
-        launch(left_copy(a))
-        launch(main_copy(a))
-    launch(twin_copy(0, 0))
+        return held[a, b, c, flag_row:head, :].astype(jnp.float32)
+
+    def spread(a):
+        low = a & -a if a else steps
+        for bit in reversed(hops):
+            if bit < low:
+                launch(main_copy(a + bit))
+                launch(left_copy(a + bit))
+        launch(side_copy(a))
+        launch(twin_copy(a, 0))
+
+    spread(0)
     flags = absorb(0, 0, 0)
 
     for load in loads[8:]:
@@ -213,10 +238,9 @@
     weight_t[...] = outer[:, 0:pair].astype(jnp.float32).T.astype(jnp.bfloat16)
 
     for a in range(1, steps):
-        left_copy(steps - a).wait_recv()
-        main_copy(steps - a).wait_recv()
-        launch(side_copy(a))
-        launch(twin_copy(a, 0))
+        main_copy(a).wait_recv()
+        left_copy(a).wait_recv()
+        spread(a)
         flags = flags + absorb(a, 0, 0)
     for a in range(steps):
         side_copy(a).wait_recv()
@@ -297,7 +321,7 @@
     pair = out_weight.shape[1]
     rows_here = residues // devices
     block_rows = seqs * channels
-    total_rows = 4 * rows_here + TILE + block_rows * (residues // LANES)
+    total_rows = residues + TILE + block_rows * (residues // LANES)
     operands = [
         alignment,
         norm_gain.reshape(1, -1),

time: 18.8 us -> 20.6 us (1.096)
  Pallas kernels: 16.9 us -> 18.7 us
    pallas_call x1, Pallas kernels: 16.9 us -> 18.7 us  [per_device(): pl.pallas_call(functools.partial(kernel, steps), out_shape=jax.ShapeDtype...]
where the time goes in v3:
time: 20.6 us; the launch traced here: 20.4 us
  Pallas kernels  18.7 us (91%)
  local copies, waits for them, and re-layouts  1.67 us (8%)
    pallas_call x1, Pallas kernels, per_device(): pl.pallas_call(functools.partial(kernel, steps), out_shape=jax.ShapeDtype...  18.7 us
    unnamed x1, local copies, waits for them, and re-layouts  1.67 us

profile of v3, /device:TPU:1, one launch (start us, length us, event | category | flops | bytes accessed | tf_op | source)
XLA Modules:
  0.0 20.4 jit_solution(18176562735252440116)
XLA Ops:
  0.0 18.7 %shard_map.109 = bf16[8,128,128]{2,1,0:T(8,128)(2,1)} custom-call(bf16[4,128,256]{2,1,0:T(8,128)(2,1)} %refs_0_.1, f32[1,256]{1,0:T(1,128)} %bitcast.11, f32[1,256]{1,0:T(1,128)} %bitcast.12, bf16[32,256]{1,0:T(8,128)(2,1)} %bitcast.8, f32[1,32]{1,0:T(1,128)} %bitcast.13, bf16[32,256]{1,0:T(8,128)(2,1)} %bitcast.9, f32[1,32]{1,0:T(1,128)} %bitcast.14, ...), custom_call_target="tpu_custom_call" | custom-call | tf_op jit(solution)/shard_map/pallas_call | solution.py:341
  18.7 1.7 %copy.13 = bf16[8,128,128]{2,1,0:T(8,128)(2,1)} copy(bf16[8,128,128]{2,1,0:T(8,128)(2,1)} %shard_map.109) | data formatting | bytes 524288
